TPU v7x, 32 devices: a whole 2x2x4 slice. The times are simulated.
32 devices in a mesh: dp: 8 (over z, x), fsdp: 4 (over y, core).
Axes of the slice: x: 2, y: 2, z: 4, core: 2. Of those that a mesh axis runs over, the one named last changes fastest.
Arguments:
- tokens: bfloat16 [32, 1024, 768], P(('dp', 'fsdp')), may hold values from -11 to 11
- lengths: int32 [32], P(('dp', 'fsdp')), may hold values from 256 to 1024, as said below
- buckets: int32 [2047], replicated, may hold values from 0 to 31
- rel_table: float32 [32, 12], replicated, may hold values from -4 to 4
- gain_attn: float32 [768], replicated, may hold values from 0.5 to 1.5
- gain_ff: float32 [768], replicated, may hold values from 0.5 to 1.5
- w_qkv: bfloat16 [768, 2304], replicated, may hold values from -0.21875 to 0.21875
- w_out: bfloat16 [768, 768], replicated, may hold values from -0.875 to 0.875
- w_in: bfloat16 [768, 3072], replicated, may hold values from -0.21875 to 0.21875
- w_down: bfloat16 [3072, 768], replicated, may hold values from -0.109375 to 0.109375
- adapters: bfloat16 [622080], P(('dp', 'fsdp')), may hold values from -5 to 5
- cotangent: bfloat16 [32, 1024, 768], P(('dp', 'fsdp')), may hold values from -6 to 6
Outputs:
- block_out: bfloat16 [32, 1024, 768], P(('dp', 'fsdp'))
- tokens_grad: float32 [32, 1024, 768], P(('dp', 'fsdp'))
- adapters_grad: float32 [622080], P(('dp', 'fsdp'))
- root_squares: float32 [4], replicated
Inputs may be any that keep to these rules, and one draw needn't show every extreme that they name: `lengths`: each sequence's count of valid leading positions; in every draw one sequence has all 1024.
All inputs are finite; a program needn't handle non-finite values.
Results may differ from a plain program's by a relative error of at most 0.017.
Values may be sent and summed in bfloat16 or wider, within the bound.
A program may use at most 512 MiB of HBM per device.

v0:
```python
import functools

import jax
import jax.numpy as jnp
from jax import lax
from jax.experimental import pallas as pl
from jax.experimental.pallas import tpu as pltpu
from jax.sharding import PartitionSpec as P

D = 768
FF = 3072
HEADS = 12
HDIM = 64
EXPERTS = 10
RANK = 4
FANS = ((D, D), (D, D), (D, D), (D, D), (D, FF), (FF, D))
COLS = EXPERTS * RANK
LANES = 128

EPSILON = 1e-06
MASKED = -1000000000.0
GELU_SCALE = 0.7978845608028654
GELU_CUBIC = 0.044715
LOG2E = 1.4426950408889634
LN2 = 0.6931471805599453
QUERY_SCALE = 0.125 * LOG2E

ROWS = 256
MIDDLE_ROWS = 512
CHUNK = 512
QBLOCK = 256
UP_ROWS = 48
DOWN_ROWS = 2 * COLS
VMEM_BYTES = 60 * 1024 * 1024

F32 = jnp.float32
BF16 = jnp.bfloat16


def dot(a, b):
    return lax.dot_general(a, b, (((1,), (0,)), ((), ())), preferred_element_type=F32)


def dot_nt(a, b):
    return lax.dot_general(a, b, (((1,), (1,)), ((), ())), preferred_element_type=F32)


def dot_tn(a, b):
    return lax.dot_general(a, b, (((0,), (0,)), ((), ())), preferred_element_type=F32)


def lane_iota(shape):
    return lax.broadcasted_iota(jnp.int32, shape, 1)


def row_iota(shape):
    return lax.broadcasted_iota(jnp.int32, shape, 0)


def gates_of(logits):
    weights = jnp.exp(logits - jnp.max(logits, axis=0, keepdims=True))
    return weights * (4.0 / jnp.sum(weights, axis=0, keepdims=True))


def gate_grads(grad_mixed, lowrank, gates):
    product = grad_mixed * lowrank
    summed = product
    for step in range(1, RANK):
        summed = summed + pltpu.roll(product, COLS - step, 0)
    centre = jnp.sum(gates * product, axis=0, keepdims=True)
    first = row_iota(gates.shape) % RANK == 0
    return grad_mixed * gates, jnp.where(first, gates * (summed - centre), 0.0)


def pad_rows(value, rows):
    return jnp.concatenate([value, jnp.zeros((rows - value.shape[0], value.shape[1]), F32)], axis=0)


def single_gates(packed):
    turned = packed.T
    lowrank = turned[:COLS]
    gates = gates_of(turned[COLS : 2 * COLS])
    mixed = pad_rows(lowrank * gates, LANES).astype(BF16)
    return lowrank, gates, mixed, mixed.T


def single_deltas(grad_mixed, lowrank, gates):
    parts = gate_grads(grad_mixed.T[:COLS], lowrank, gates)
    delta = pad_rows(jnp.concatenate(parts, axis=0), LANES).astype(BF16)
    return delta, delta.T


def rms_inverse(values):
    return lax.rsqrt(jnp.mean(values * values, axis=-1, keepdims=True) + EPSILON)


def rms_backward(values, gain, inverse, grad_normed):
    weighted = grad_normed * gain
    return inverse * weighted - values * (
        inverse * inverse * inverse * jnp.mean(values * weighted, axis=-1, keepdims=True)
    )


def params(**more):
    return pltpu.CompilerParams(vmem_limit_bytes=VMEM_BYTES, **more)


def whole(shape):
    zeros = (0,) * len(shape)
    return pl.BlockSpec(shape, lambda *_: zeros, pipeline_mode=pl.Buffered(1))


def bias_table(offset_row, length):
    spread = jnp.broadcast_to(offset_row, (LANES, 2 * length))
    return pltpu.roll(spread, 2 * length - (LANES - 1), 1, stride=1, stride_axis=0)


def add_bias(scores, table_ref, start, length):
    width = scores.shape[1]
    parts = []
    for block in range(length // LANES):
        offset = start - LANES * block + (length - LANES)
        parts.append(
            scores[block * LANES : (block + 1) * LANES] + table_ref[:, offset : offset + width]
        )
    return jnp.concatenate(parts, axis=0)


def key_extras(length_ref, shape, odd):
    lane = lane_iota(shape) - (0 if odd else HDIM)
    invalid = row_iota(shape) >= length_ref[0]
    extras = jnp.where((lane == 0) & invalid, MASKED, 0.0)
    return jnp.where((lane >= 1) & (lane <= 3), 1.0, extras).astype(BF16)


def head_lanes(odd):
    lane = lane_iota((1, LANES))
    return ((lane >= HDIM) if odd else (lane < HDIM)).astype(F32).astype(BF16)


def extra_rows(rows):
    width = rows[0].shape[1]
    index = row_iota((8, width))
    block = jnp.zeros((8, width), F32)
    for place, row in enumerate(rows):
        block = jnp.where(index == place, row, block)
    return jnp.concatenate([block, jnp.zeros((HDIM - 8, width), F32)], axis=0).astype(BF16)


def split_three(row):
    high = row.astype(BF16).astype(F32)
    middle = (row - high).astype(BF16).astype(F32)
    return high, middle, row - high - middle


def join_rows(rows, extras, odd):
    return jnp.concatenate([extras, rows] if odd else [rows, extras], axis=0)


def attend_kernel(
    length_ref, off_ref, qt_ref, k_ref, kt_ref, vt_ref, o_ref, lse_ref, table, key_more, plain
):
    length = k_ref.shape[0]
    step = pl.program_id(0)

    @pl.when(step == 0)
    def _():
        for odd in range(2):
            key_more[odd] = key_extras(length_ref, k_ref.shape, odd)

    starts = range(0, length, QBLOCK)
    ones = jnp.ones((1, length), F32)

    def half_of(odd):
        return slice(odd * HDIM, (odd + 1) * HDIM)

    def keys_of(odd):
        return k_ref[...] * head_lanes(odd) + key_more[odd]

    def values_of(odd):
        return jnp.concatenate([vt_ref[half_of(odd), :], jnp.ones((16, length), BF16)], axis=0)

    def finish(odd, start, shift, weights):
        columns = slice(start, start + QBLOCK)
        summed = dot(values_of(odd), weights)
        total = summed[HDIM : HDIM + 1]
        o_ref[half_of(odd), columns] = (summed[:HDIM] / total).astype(BF16)
        lse_ref[0, odd : odd + 1, columns] = shift + jnp.log2(total)
        return total

    def bounded(odd):
        offsets = off_ref[pl.ds(2 * step + odd, 1), :]
        table[odd] = bias_table(offsets, length)
        squares = jnp.square(kt_ref[half_of(odd), :].astype(F32))
        sizes = jnp.sum(squares, axis=0, keepdims=True)
        sizes = jnp.where(lane_iota(sizes.shape) < length_ref[0], sizes, 0.0)
        largest = jnp.max(sizes, axis=1, keepdims=True)
        rows = qt_ref[half_of(odd), :].astype(F32)
        norms = jnp.sqrt(jnp.sum(rows * rows, axis=0, keepdims=True) * largest)
        bound = 1.001 * norms + jnp.max(offsets, axis=1, keepdims=True)
        queries = join_rows(
            qt_ref[half_of(odd), :],
            extra_rows([ones] + [-part for part in split_three(bound)]),
            odd,
        )
        keys = keys_of(odd)
        scores = [dot(keys, queries[:, start : start + QBLOCK]) for start in starts]
        weights = [
            jnp.exp2(add_bias(part, table.at[odd], start, length)).astype(BF16)
            for part, start in zip(scores, starts)
        ]
        least = None
        for start, part in zip(starts, weights):
            total = finish(odd, start, bound[:, start : start + QBLOCK], part)
            least = total if least is None else jnp.minimum(least, total)
        return least

    def exact(odd):
        plain[...] = join_rows(qt_ref[half_of(odd), :], extra_rows([ones]), odd)
        keys = keys_of(odd)

        def block(index, _):
            columns = pl.ds(pl.multiple_of(index * LANES, LANES), LANES)
            raw = dot(keys, plain[:, columns])
            parts = []
            for row in range(0, length, LANES):
                place = pl.multiple_of(index * LANES - row + (length - LANES), LANES)
                parts.append(raw[row : row + LANES] + table[odd, :, pl.ds(place, LANES)])
            scores = jnp.concatenate(parts, axis=0)
            peak = jnp.max(scores, axis=0, keepdims=True)
            summed = dot(values_of(odd), jnp.exp2(scores - peak).astype(BF16))
            total = summed[HDIM : HDIM + 1]
            o_ref[half_of(odd), columns] = (summed[:HDIM] / total).astype(BF16)
            lse_ref[0, odd : odd + 1, columns] = peak + jnp.log2(total)
            return 0

        lax.fori_loop(0, length // LANES, block, 0)

    least = jnp.minimum(bounded(0), bounded(1))

    @pl.when(jnp.logical_not(jnp.min(least) > 2.0**-100))
    def _():
        for odd in range(2):
            exact(odd)


def attend(length_valid, offsets, qt, k, kt, vt):
    length = k.shape[0]
    turned = pl.BlockSpec((LANES, length), lambda p: (p, 0))
    natural = pl.BlockSpec((length, LANES), lambda p: (0, p))
    return pl.pallas_call(
        attend_kernel,
        grid=(HEADS // 2,),
        in_specs=[
            pl.BlockSpec(memory_space=pltpu.SMEM),
            whole(offsets.shape),
            turned,
            natural,
            turned,
            turned,
        ],
        out_specs=[turned, pl.BlockSpec((1, 2, length), lambda p: (p, 0, 0))],
        out_shape=[
            jax.ShapeDtypeStruct((D, length), BF16),
            jax.ShapeDtypeStruct((HEADS // 2, 2, length), F32),
        ],
        scratch_shapes=[
            pltpu.VMEM((2, LANES, 2 * length), F32),
            pltpu.VMEM((2, length, LANES), BF16),
            pltpu.VMEM((LANES, length), BF16),
        ],
        compiler_params=params(),
        name="attend",
    )(length_valid, offsets, qt, k, kt, vt)


def middle_kernel(
    length_ref,
    ot_ref,
    x_ref,
    cot_ref,
    gain_ref,
    w_out_ref,
    w_in_hbm,
    w_down_hbm,
    ar_out_ref,
    b_out_ref,
    ar_in_ref,
    b_in_ref,
    ar_down_ref,
    b_down_ref,
    out_ref,
    dmid_ref,
    gt_ref,
    sums_ref,
    dar_out_ref,
    db_out_ref,
    dar_in_ref,
    db_in_ref,
    dar_down_ref,
    db_down_ref,
    active,
    slope,
    sloped,
    grad_hidden,
    feeds,
    w_in_ref,
    w_down_ref,
    loaded,
):
    step = pl.program_id(0)
    loads = [
        pltpu.make_async_copy(w_in_hbm, w_in_ref, loaded.at[0]),
        pltpu.make_async_copy(w_down_hbm, w_down_ref, loaded.at[1]),
    ]

    @pl.when(step == 0)
    def _():
        for load in loads:
            load.start()
        for ref in (
            sums_ref,
            dar_out_ref,
            db_out_ref,
            dar_in_ref,
            db_in_ref,
            dar_down_ref,
            db_down_ref,
        ):
            ref[...] = jnp.zeros_like(ref)

    attended = ot_ref[...].T
    inputs = x_ref[...].astype(F32)
    gain = gain_ref[...].reshape(1, D)
    cot = cot_ref[...]

    packed_out = dot(attended, ar_out_ref[...])
    branch = dot(attended, w_out_ref[...])
    low_out, gates_out, mixed_out, natural = single_gates(packed_out)
    grad_mixed_down = dot_nt(cot, b_down_ref[...])
    branch = branch + dot(natural, b_out_ref[...])
    middle = inputs + branch
    inverse = rms_inverse(middle)
    normed = (middle * inverse * gain).astype(BF16)

    packed_in = dot(normed, ar_in_ref[...])
    low_in, gates_in, mixed_in, natural = single_gates(packed_in)

    def columns_of(index):
        return pl.ds(pl.multiple_of(index * CHUNK, CHUNK), CHUNK)

    def hidden_of(chunk):
        return dot(normed, w_in_ref[:, chunk]) + dot(natural, b_in_ref[:, chunk])

    def activate(chunk, values):
        grad_dense = dot_nt(cot, w_down_ref[chunk])
        square = values * values
        tangent = jnp.tanh(values * (GELU_SCALE + (GELU_SCALE * GELU_CUBIC) * square))
        half = 0.5 + 0.5 * tangent
        smooth = values * half
        active[:, chunk] = smooth.astype(BF16)
        steep = half + smooth * (1.0 - tangent) * (
            GELU_SCALE + (3.0 * GELU_SCALE * GELU_CUBIC) * square
        )
        slope[:, chunk] = steep.astype(BF16)
        sloped[:, chunk] = grad_dense * steep

    def forward_pair(pair, _):
        chunk_a = columns_of(2 * pair)
        chunk_b = columns_of(2 * pair + 1)
        hidden_a = hidden_of(chunk_a)
        hidden_b = hidden_of(chunk_b)
        activate(chunk_a, hidden_a)
        activate(chunk_b, hidden_b)
        return 0

    @pl.when(step == 0)
    def _():
        for load in loads:
            load.wait()

    lax.fori_loop(0, FF // (2 * CHUNK), forward_pair, 0)

    packed_down = dot(active[...], ar_down_ref[...])
    for first in range(0, D, 256):
        part = slice(first, first + 256)
        feeds[:, part] = dot(active[...], w_down_ref[:, part])
    feed = feeds[...]
    low_down, gates_down, mixed_down, natural = single_gates(packed_down)
    delta_down, natural_delta = single_deltas(grad_mixed_down, low_down, gates_down)
    db_down_ref[...] += dot(mixed_down[:UP_ROWS], cot)
    feed = feed + dot(natural, b_down_ref[...])
    output = middle + feed
    out_ref[...] = output.astype(BF16)

    for first in range(0, FF, CHUNK):
        chunk = slice(first, first + CHUNK)
        grad_low = dot_nt(natural_delta, ar_down_ref[chunk])
        grad_hidden[:, chunk] = (
            sloped[:, chunk] + grad_low * slope[:, chunk].astype(F32)
        ).astype(BF16)

    rows = row_iota((MIDDLE_ROWS, 1)) + step * MIDDLE_ROWS
    valid = (rows < length_ref[0]).astype(F32)
    lane = lane_iota((8, LANES))
    totals = jnp.where((lane == 4) & (step == 0), length_ref[0].astype(F32), 0.0)
    for place, member in enumerate((inputs, branch, feed, output)):
        kept = member * valid
        totals = jnp.where(lane == place, jnp.sum(kept * kept), totals)
    sums_ref[...] += totals

    grad_mixed = dot_nt(grad_hidden[...], b_in_ref[...])
    for first in range(0, D, 256):
        part = slice(first, first + 256)
        feeds[:, part] = dot_nt(grad_hidden[...], w_in_ref[part])
    grad_normed = feeds[...]
    delta_in, natural_delta = single_deltas(grad_mixed, low_in, gates_in)
    grad_normed = grad_normed + dot_nt(natural_delta, ar_in_ref[...])
    dar_in_ref[...] += dot(delta_in[:DOWN_ROWS], normed)

    grad_middle = cot.astype(F32) + rms_backward(middle, gain, inverse, grad_normed)
    dmid_ref[...] = grad_middle
    grad_branch = grad_middle.astype(BF16)
    grad_mixed = dot_nt(grad_branch, b_out_ref[...])
    grad_attended = dot_nt(grad_branch, w_out_ref[...])
    dar_down_ref[...] += dot(delta_down[:DOWN_ROWS], active[...])
    db_in_ref[...] += dot(mixed_in[:UP_ROWS], grad_hidden[...])
    delta_out, natural_delta = single_deltas(grad_mixed, low_out, gates_out)
    grad_attended = grad_attended + dot_nt(natural_delta, ar_out_ref[...])
    gt_ref[...] = grad_attended.astype(BF16).T
    dar_out_ref[...] += dot(delta_out[:DOWN_ROWS], attended)
    db_out_ref[...] += dot(mixed_out[:UP_ROWS], grad_branch)


def middle_part(length_valid, ot, x, cot, gain, w_out, w_in, w_down, adapters):
    length = x.shape[0]
    tile = pl.BlockSpec((MIDDLE_ROWS, D), lambda i: (i, 0))
    turned = pl.BlockSpec((D, MIDDLE_ROWS), lambda i: (0, i))
    grad_shapes = [
        jax.ShapeDtypeStruct(shape, F32)
        for fan_in, fan_out in FANS[3:]
        for shape in ((DOWN_ROWS, fan_in), (UP_ROWS, fan_out))
    ]
    out_shape = [
        jax.ShapeDtypeStruct((length, D), BF16),
        jax.ShapeDtypeStruct((length, D), F32),
        jax.ShapeDtypeStruct((D, length), BF16),
        jax.ShapeDtypeStruct((8, LANES), F32),
    ] + grad_shapes
    return pl.pallas_call(
        middle_kernel,
        grid=(length // MIDDLE_ROWS,),
        in_specs=[pl.BlockSpec(memory_space=pltpu.SMEM), turned, tile, tile]
        + [whole(gain.shape), whole(w_out.shape)]
        + [pl.BlockSpec(memory_space=pl.ANY)] * 2
        + [whole(member.shape) for member in adapters],
        out_specs=[tile, tile, turned] + [whole(member.shape) for member in out_shape[3:]],
        out_shape=out_shape,
        scratch_shapes=[
            pltpu.VMEM((MIDDLE_ROWS, FF), BF16),
            pltpu.VMEM((MIDDLE_ROWS, FF), BF16),
            pltpu.VMEM((MIDDLE_ROWS, FF), F32),
            pltpu.VMEM((MIDDLE_ROWS, FF), BF16),
            pltpu.VMEM((MIDDLE_ROWS, D), F32),
            pltpu.VMEM(w_in.shape, BF16),
            pltpu.VMEM(w_down.shape, BF16),
            pltpu.SemaphoreType.DMA((2,)),
        ],
        compiler_params=params(),
        name="middle_part",
    )(length_valid, ot, x, cot, gain, w_out, w_in, w_down, *adapters)


def attend_back(
    pair,
    length_ref,
    off_ref,
    qt_ref,
    k_ref,
    kt_ref,
    v_ref,
    ot_ref,
    gt_ref,
    lse_ref,
    grads_ref,
    table,
    key_more,
    weights_all,
    grads_all,
):
    length = k_ref.shape[0]
    lane = lane_iota((1, LANES))
    first_lanes = lane < HDIM
    grad_query_parts = []
    for odd in range(2):
        half = slice(odd * HDIM, (odd + 1) * HDIM)
        table[odd] = bias_table(off_ref[pl.ds(2 * pair + odd, 1), :], length)
        keys = k_ref[...] * head_lanes(odd) + key_more[odd]
        place = lane - (0 if odd else HDIM)
        value_more = ((place >= 0) & (place < 3)).astype(F32).astype(BF16)
        values = v_ref[...] * head_lanes(odd) + value_more
        ones = jnp.ones((1, length), F32)
        lse = lse_ref[0, odd : odd + 1, :]
        queries = join_rows(
            qt_ref[half, :], extra_rows([ones] + [-part for part in split_three(lse)]), odd
        )
        delta = jnp.sum(
            ot_ref[half, :].astype(F32) * gt_ref[half, :].astype(F32), axis=0, keepdims=True
        )
        grads = join_rows(
            gt_ref[half, :], extra_rows([-part for part in split_three(delta)]), odd
        )
        for start in range(0, length, QBLOCK):
            columns = slice(start, start + QBLOCK)
            scores = add_bias(dot(keys, queries[:, columns]), table.at[odd], start, length)
            weights = jnp.exp2(scores)
            weights_all[:, columns] = weights.astype(BF16)
            grad_scores = weights * dot(values, grads[:, columns])
            grads_all[:, columns] = grad_scores.astype(BF16)
        grad_query_parts.append(dot(kt_ref[half, :], grads_all[...]) * 0.125)
        grad_values = dot_nt(weights_all[...], gt_ref[...])
        grad_keys = dot_nt(grads_all[...], qt_ref[...]) * LN2
        if odd:
            grad_values = jnp.where(first_lanes, even_values, grad_values)
            grad_keys = jnp.where(first_lanes, even_keys, grad_keys)
        else:
            even_values, even_keys = grad_values, grad_keys
    columns = pl.ds(pl.multiple_of(pair * LANES, LANES), LANES)
    grads_ref[0, :, columns] = jnp.concatenate(grad_query_parts, axis=0).T.astype(BF16)
    grads_ref[1, :, columns] = grad_keys.astype(BF16)
    grads_ref[2, :, columns] = grad_values.astype(BF16)


def project_back(
    tile, x_ref, gain_ref, w_ref, ar_ref, b_ref, zg_ref, grads_ref, dmid_ref, out_ref, dar_ref, db_ref
):
    values = x_ref[...].astype(F32)
    gain = gain_ref[...].reshape(1, D)
    inverse = rms_inverse(values)
    normed = (values * inverse * gain).astype(BF16)
    lowrank = zg_ref[: 3 * COLS]
    gates = zg_ref[3 * COLS :]
    mixed = pad_rows(lowrank * gates, LANES).astype(BF16)
    rows = pl.ds(pl.multiple_of(tile * ROWS, ROWS), ROWS)
    grads = [grads_ref[index, rows] for index in range(3)]
    columns = [slice(index * D, (index + 1) * D) for index in range(3)]
    grad_mixed = jnp.zeros((ROWS, LANES), F32)
    for grad, lanes in zip(grads, columns):
        grad_mixed = grad_mixed + dot_nt(grad, b_ref[:, lanes])
    grad_normed = jnp.zeros((ROWS, D), F32)
    for grad, lanes in zip(grads, columns):
        grad_normed = grad_normed + dot_nt(grad, w_ref[:, lanes])
        db_ref[:, lanes] += dot(mixed, grad)
    turned = grad_mixed.T
    parts = []
    for first in range(0, 3 * COLS, COLS):
        place = slice(first, first + COLS)
        parts.append(gate_grads(turned[place], lowrank[place], gates[place]))
    delta = jnp.concatenate([part[0] for part in parts] + [part[1] for part in parts], axis=0)
    delta = pad_rows(delta, 2 * LANES).astype(BF16)
    grad_normed = grad_normed + dot_nt(delta.T, ar_ref[...])
    dar_ref[...] += dot(delta, normed)
    out_ref[...] = dmid_ref[...] + rms_backward(values, gain, inverse, grad_normed)


def back_kernel(*refs):
    length_ref = refs[0]
    heads_refs = refs[:9]
    x_ref, gain_ref, w_hbm, ar_ref, b_ref, zg_ref, dmid_ref = refs[9:16]
    out_ref, dar_ref, db_ref = refs[16:19]
    table, key_more, weights_all, grads_all, grads_ref, w_ref, loaded = refs[19:]
    step = pl.program_id(0)
    pairs = HEADS // 2
    load = pltpu.make_async_copy(w_hbm, w_ref, loaded)

    @pl.when(step == 0)
    def _():
        load.start()
        dar_ref[...] = jnp.zeros_like(dar_ref)
        db_ref[...] = jnp.zeros_like(db_ref)
        for odd in range(2):
            key_more[odd] = key_extras(length_ref, key_more.shape[1:], odd)

    @pl.when(step < pairs)
    def _():
        attend_back(step, *heads_refs, grads_ref, table, key_more, weights_all, grads_all)

    @pl.when(step == pairs)
    def _():
        load.wait()

    @pl.when(step >= pairs)
    def _():
        project_back(
            step - pairs,
            x_ref,
            gain_ref,
            w_ref,
            ar_ref,
            b_ref,
            zg_ref,
            grads_ref,
            dmid_ref,
            out_ref,
            dar_ref,
            db_ref,
        )


def back_part(
    length_valid, offsets, qt, k, kt, v, ot, gt, lse, x, gain, w_qkv, ar_qkv, b_qkv, zg, dmid
):
    length = k.shape[0]
    pairs = HEADS // 2

    def pair_of(i):
        return jnp.minimum(i, pairs - 1)

    def tile_of(i):
        return jnp.maximum(i - pairs, 0)

    turned = pl.BlockSpec((LANES, length), lambda i: (pair_of(i), 0))
    natural = pl.BlockSpec((length, LANES), lambda i: (0, pair_of(i)))
    tile = pl.BlockSpec((ROWS, D), lambda i: (tile_of(i), 0))
    out_shape = [
        jax.ShapeDtypeStruct((length, D), F32),
        jax.ShapeDtypeStruct((2 * LANES, D), F32),
        jax.ShapeDtypeStruct((LANES, 3 * D), F32),
    ]
    return pl.pallas_call(
        back_kernel,
        grid=(pairs + length // ROWS,),
        in_specs=[
            pl.BlockSpec(memory_space=pltpu.SMEM),
            whole(offsets.shape),
            turned,
            natural,
            turned,
            natural,
            turned,
            turned,
            pl.BlockSpec((1, 2, length), lambda i: (pair_of(i), 0, 0)),
            tile,
            whole((D,)),
            pl.BlockSpec(memory_space=pl.ANY),
            whole(ar_qkv.shape),
            whole(b_qkv.shape),
            pl.BlockSpec((6 * COLS, ROWS), lambda i: (0, tile_of(i))),
            tile,
        ],
        out_specs=[tile] + [whole(member.shape) for member in out_shape[1:]],
        out_shape=out_shape,
        scratch_shapes=[
            pltpu.VMEM((2, LANES, 2 * length), F32),
            pltpu.VMEM((2, length, LANES), BF16),
            pltpu.VMEM((length, length), BF16),
            pltpu.VMEM((length, length), BF16),
            pltpu.VMEM((3, length, D), BF16),
            pltpu.VMEM(w_qkv.shape, BF16),
            pltpu.SemaphoreType.DMA,
        ],
        compiler_params=params(),
        name="back_part",
    )(length_valid, offsets, qt, k, kt, v, ot, gt, lse, x, gain, w_qkv, ar_qkv, b_qkv, zg, dmid)


PARAM_ROWS = sum((COLS + EXPERTS) * fan_in + COLS * fan_out for fan_in, fan_out in FANS) // LANES


def piece_rows():
    result = []
    row = 0
    for fan_in, fan_out in FANS:
        starts = []
        for count in (fan_in * COLS, COLS * fan_out, fan_in * EXPERTS):
            starts.append(row)
            row += count // LANES
        result.append(tuple(starts))
    return result


def shard_rows(count):
    return -(-count // (LANES * 16)) * 16


def align_in(flat_ref, shard, start):
    first, shift = divmod(start, LANES)
    rows = shard.shape[0]
    if shift == 0:
        flat_ref[first : first + rows] = shard
        return
    turned = pltpu.roll(shard, shift, 1)
    lane = lane_iota((1, LANES))
    zeros = jnp.zeros((8, LANES), F32)
    upper = jnp.concatenate([turned, zeros], axis=0)
    lower = pltpu.roll(upper, 1, 0)
    kept = flat_ref[first : first + 8]
    merged = jnp.where(lane >= shift, upper, lower)
    inside = (row_iota((8, LANES)) == 0) & (lane_iota((8, LANES)) < shift)
    flat_ref[first : first + 8] = jnp.where(inside, kept, merged[:8])
    flat_ref[first + 8 : first + 8 + rows] = merged[8:]


def align_out(flat_ref, rows, start):
    first, shift = divmod(start, LANES)
    if shift == 0:
        return flat_ref[first : first + rows]
    block = flat_ref[first : first + rows + 8]
    turned = pltpu.roll(block, LANES - shift, 1)
    below = pltpu.roll(turned, rows + 7, 0)
    lane = lane_iota((1, LANES))
    return jnp.where(lane < LANES - shift, turned, below)[:rows]


GROUP = 64


def narrow_to_rows(flat_ref, fan_in, items, out_ref, begin=0):
    groups = fan_in // GROUP
    lane = lane_iota((1, LANES))
    lines = [
        [
            flat_ref[pl.ds(base + k, groups, stride=width * GROUP // LANES), :]
            for k in range(width * GROUP // LANES)
        ]
        for base, width, _ in items
    ]
    for b in range(GROUP):
        result = jnp.zeros((groups, LANES), F32)
        for line, (_, width, place) in zip(lines, items):
            first, shift = divmod(width * b, LANES)
            amount = (place - shift) % LANES
            value = line[first] if amount == 0 else pltpu.roll(line[first], amount, 1)
            if shift + width > LANES:
                value = jnp.where(
                    lane < place + LANES - shift, value, pltpu.roll(line[first + 1], amount, 1)
                )
            inside = (lane >= place) & (lane < place + width)
            result = jnp.where(inside, value, result)
        out_ref[pl.ds(begin + b, groups, stride=GROUP), :] = result


def rows_to_narrow(in_ref, fan_in, items, flat_ref, begin=0):
    groups = fan_in // GROUP
    lane = lane_iota((1, LANES))
    lines = [
        [jnp.zeros((groups, LANES), F32) for _ in range(width * GROUP // LANES)]
        for _, width, _ in items
    ]
    for b in range(GROUP):
        source = in_ref[pl.ds(begin + b, groups, stride=GROUP), :]
        for line, (_, width, place) in zip(lines, items):
            first, shift = divmod(width * b, LANES)
            amount = (shift - place) % LANES
            value = source if amount == 0 else pltpu.roll(source, amount, 1)
            inside = (lane >= shift) & (lane < shift + width)
            line[first] = jnp.where(inside, value, line[first])
            if shift + width > LANES:
                line[first + 1] = jnp.where(lane < shift + width - LANES, value, line[first + 1])
    for line, (base, width, _) in zip(lines, items):
        for k, value in enumerate(line):
            flat_ref[pl.ds(base + k, groups, stride=width * GROUP // LANES), :] = value


def single_items(block):
    starts = piece_rows()
    after_out, after_in = (block + 4) // 5, (block + 2) // 4
    down = (block - 2) * after_in
    bases = []
    for piece, width in ((0, COLS), (2, EXPERTS)):
        out, inner, outer = (starts[index][piece] for index in range(3, 6))
        base = out + (inner - out) * after_out + (outer - inner) * after_in
        bases.append(base + down * (D * width // LANES))
    return [(bases[0], COLS, 0), (bases[1], EXPERTS, COLS)]


SINGLE_BLOCKS = 2 + FF // D


def spread_matrix(experts, source, place):
    row = row_iota((LANES, LANES)) - source
    lane = lane_iota((LANES, LANES)) - place
    hit = (lane >= RANK * row) & (lane < RANK * row + RANK) & (row >= 0) & (row < experts)
    return jnp.where(hit, 1.0, 0.0)


def keep_matrix():
    row = row_iota((LANES, LANES))
    return jnp.where((row == lane_iota((LANES, LANES))) & (row < COLS), 1.0, 0.0)


FIRST_COUNT = sum((COLS + EXPERTS) * fan_in + COLS * fan_out for fan_in, fan_out in FANS[:3])


def unpack_ups(flat, base, fan_out, first, out_ref, column):
    width = fan_out // LANES
    above = jnp.zeros((first, LANES), F32)
    below = jnp.zeros((LANES - COLS - first, LANES), F32)
    for k in range(width):
        part = flat[pl.ds(base + k, COLS, stride=width), :]
        parts = [part, below] if first == 0 else [above, part, below]
        lanes = slice(column + k * LANES, column + (k + 1) * LANES)
        out_ref[:, lanes] = jnp.concatenate(parts, axis=0).astype(BF16)


def unpack_first(flat, ar_ref, b_ref, down, router):
    starts = piece_rows()
    narrow_to_rows(flat, D, [(starts[k][0], COLS, k * COLS) for k in range(3)], down)
    narrow_to_rows(flat, D, [(starts[k][2], EXPERTS, k * EXPERTS) for k in range(3)], router)
    routers = router[...].astype(BF16)
    for half in range(2):
        matrix = spread_matrix(3 * EXPERTS, 0, 3 * COLS - half * LANES).astype(BF16)
        packed = dot(routers, matrix)
        packed = packed if half else packed + down[...]
        ar_ref[:, half * LANES : (half + 1) * LANES] = packed.astype(BF16)
    for index in range(3):
        unpack_ups(flat, starts[index][1], D, index * COLS, b_ref, index * D)


def flat_rows(count):
    return PARAM_ROWS + shard_rows(count) + 20


def unpack_rest(flat, outs, work):
    starts = piece_rows()
    matrix = (keep_matrix() + spread_matrix(EXPERTS, COLS, COLS)).astype(BF16)

    def block(index, _):
        narrow_to_rows(flat, D, single_items(index), work, index * D)
        return 0

    lax.fori_loop(0, SINGLE_BLOCKS, block, 0)
    begin = 0
    for index in range(3, 6):
        fan_in, fan_out = FANS[index]
        ar_ref, b_ref = outs[2 * index - 6], outs[2 * index - 5]
        ar_ref[...] = dot(work[begin : begin + fan_in].astype(BF16), matrix).astype(BF16)
        unpack_ups(flat, starts[index][1], fan_out, 0, b_ref, 0)
        begin += fan_in


def split_dot(value, matrix):
    high = value.astype(BF16)
    return dot(high, matrix) + dot((value - high.astype(F32)).astype(BF16), matrix)


def first_of_four(experts, source, place):
    row = row_iota((LANES, LANES)) - source
    lane = lane_iota((LANES, LANES)) - place
    hit = (row == RANK * lane) & (lane >= 0) & (lane < experts)
    return jnp.where(hit, 1.0, 0.0)


def assemble_ups(flat, base, fan_out, first, grad_ref, column):
    width = fan_out // LANES
    for k in range(width):
        lanes = slice(column + k * LANES, column + (k + 1) * LANES)
        flat[pl.ds(base + k, COLS, stride=width), :] = grad_ref[first : first + COLS, lanes]


def assemble_rest(flat, grads, work):
    starts = piece_rows()
    matrix = (keep_matrix() + first_of_four(EXPERTS, COLS, COLS)).astype(BF16)
    begin = 0
    for index in range(3, 6):
        fan_in, fan_out = FANS[index]
        dar_ref, db_ref = grads[2 * index - 6], grads[2 * index - 5]
        work[begin : begin + fan_in] = split_dot(pad_rows(dar_ref[...], LANES).T, matrix)
        assemble_ups(flat, starts[index][1], fan_out, 0, db_ref, 0)
        begin += fan_in

    def block(index, _):
        rows_to_narrow(work, D, single_items(index), flat, index * D)
        return 0

    lax.fori_loop(0, SINGLE_BLOCKS, block, 0)


def assemble_first(flat, dar_ref, db_ref, down, router):
    starts = piece_rows()
    down[...] = dar_ref[:LANES].T
    rows_to_narrow(down, D, [(starts[k][0], COLS, k * COLS) for k in range(3)], flat)
    first_router = 3 * COLS
    turned = dar_ref[first_router : first_router + LANES].T
    router[...] = split_dot(turned, first_of_four(3 * EXPERTS, 0, 0).astype(BF16))
    rows_to_narrow(router, D, [(starts[k][2], EXPERTS, k * EXPERTS) for k in range(3)], flat)
    for index in range(3):
        assemble_ups(flat, starts[index][1], D, index * COLS, db_ref, index * D)


MESH = pl.DeviceIdType.MESH


def place_of(axes, sizes):
    me = lax.axis_index(axes[0]) * sizes[1] + lax.axis_index(axes[1])

    def coordinates(number):
        return (number // sizes[1], number % sizes[1])

    return me, coordinates


def partners_of(me):
    low = me % 8
    core = low % 2
    y = (low // 2) % 2
    x = low // 4
    over_x = low + 4 * (1 - 2 * x)
    over_y = low + 2 * (1 - 2 * y)
    first = over_x * (1 - core) + over_y * core
    second = over_y * (1 - core) + over_x * core
    both = first + second - low
    other = 1 - 2 * core
    return low, first, second, both, other, over_x, over_y


def greet(peers):
    barrier = pltpu.get_barrier_semaphore()
    for peer in peers:
        pl.semaphore_signal(barrier, inc=1, device_id=peer, device_id_type=MESH)
    pl.semaphore_wait(barrier, len(peers))


class Ring:
    def __init__(self, axes, sizes, send, receive):
        self.me, self.coordinates = place_of(axes, sizes)
        self.groups = sizes[0] * sizes[1] // 8
        self.group = self.me // 8
        places = partners_of(self.me)
        self.low, self.first, self.second, self.both, self.other, self.over_x, self.over_y = places
        self.mate = self.low + self.other
        self.send, self.receive = send, receive
        self.copies = {}

    def device(self, group, low):
        return self.coordinates(group * 8 + low)

    def greet(self):
        peers = [
            self.device((self.group + step) % self.groups, self.low)
            for step in range(1, self.groups)
        ]
        peers += [self.device(self.group, low) for low in (self.first, self.second, self.mate)]
        greet(peers)

    def copy(self, slot, source, target, peer, arrival=None):
        return pltpu.make_async_remote_copy(
            src_ref=source,
            dst_ref=target,
            send_sem=self.send.at[slot],
            recv_sem=self.receive.at[slot if arrival is None else arrival],
            device_id=peer,
            device_id_type=MESH,
        )


def gather_phases(ring, span, shard_ref, out_ref, local, greets):
    begin, end = span
    base = ring.groups
    inside = (ring.group >= begin) & (ring.group < end)

    def around(step):
        target = (ring.group + step) % ring.groups
        return ring.copy(
            step,
            shard_ref,
            out_ref.at[ring.group - begin, ring.low],
            ring.device(target, ring.low),
            base + 7 + ring.group,
        )

    def arrived(group):
        return ring.copy(
            0,
            shard_ref,
            out_ref.at[group - begin, ring.low],
            ring.device(group, ring.low),
            base + 7 + group,
        )

    def push(slot, part, partner):
        return ring.copy(
            base + slot, out_ref.at[:, part], out_ref.at[:, part], ring.device(ring.group, partner)
        )

    one = push(0, ring.low, ring.first)
    two = push(1, ring.low, ring.second)
    three = push(2, ring.first, ring.second)
    cores = [
        push(3 + index, part, ring.mate)
        for index, part in enumerate((ring.low, ring.first, ring.second, ring.both))
    ]

    def own():
        return pltpu.make_async_copy(
            shard_ref, out_ref.at[ring.group - begin, ring.low], local
        )

    def phase0():
        if greets:
            ring.greet()

        @pl.when(inside)
        def _():
            own().start()
            for step in range(1, ring.groups):
                around(step).start()

    def phase1():
        @pl.when(inside)
        def _():
            own().wait()
            for step in range(1, ring.groups):
                around(step).wait_send()

        for group in range(begin, end):

            @pl.when(ring.group != group)
            def _():
                arrived(group).wait_recv()

        for copy in (one, two, cores[0]):
            copy.start()

    def phase2():
        one.wait()
        three.start()
        cores[1].start()

    def phase3():
        two.wait()
        cores[2].start()
        three.wait()
        cores[3].start()

    def phase4():
        for copy in cores:
            copy.wait()

    return phase0, phase1, phase2, phase3, phase4


def gather_semaphores(groups):
    return [
        pltpu.SemaphoreType.DMA((groups + 7,)),
        pltpu.SemaphoreType.DMA((2 * groups + 7,)),
        pltpu.SemaphoreType.DMA,
    ]


def start_kernel(
    link,
    count,
    shard_ref,
    buckets_ref,
    table_ref,
    gain_ref,
    x_hbm,
    w_hbm,
    *refs,
):
    hbm_outs, off_ref, ar_ref, b_ref = refs[:6], refs[6], refs[7], refs[8]
    rest_refs = refs[9:15]
    x_ref, w_ref, normed, dense = refs[15:19]
    outs = refs[19:25]
    qt_ref, k_ref, kt_ref, v_ref, vt_ref, zg_ref = outs
    flat, down, router, work, loaded, stored, *more = refs[25:]
    loads = [
        pltpu.make_async_copy(x_hbm, x_ref, loaded.at[0]),
        pltpu.make_async_copy(w_hbm, w_ref, loaded.at[1]),
    ]
    stores = [
        pltpu.make_async_copy(source, target, stored.at[index])
        for index, (source, target) in enumerate(zip(outs, hbm_outs))
    ]
    for load in loads:
        load.start()
    if link is None:
        first = [lambda: None] * 5
        rest = first

        def shard_of(index):
            return shard_ref[...]
    else:
        axes, sizes, spans = link
        land_a, land_b, *sems = more
        first = gather_phases(
            Ring(axes, sizes, *sems[:2]), spans[0], shard_ref, land_a, sems[2], True
        )
        rest = gather_phases(
            Ring(axes, sizes, *sems[3:5]), spans[1], shard_ref, land_b, sems[5], False
        )

        def shard_of(index):
            group, low = divmod(index, 8)
            begin = spans[1][0]
            return land_a[group, low] if group < begin else land_b[group - begin, low]

    length = x_ref.shape[0]

    def dense_tile(index):
        rows = slice(index * length // 2, (index + 1) * length // 2)
        values = x_ref[rows].astype(F32)
        low = (values * rms_inverse(values) * gain_ref[...].reshape(1, D)).astype(BF16)
        normed[rows] = low

        def columns(part, _):
            lanes = pl.ds(pl.multiple_of(part * D, D), D)
            dense[rows, lanes] = dot(normed[rows], w_ref[:, lanes])
            return 0

        lax.fori_loop(0, 3, columns, 0)

    def project():
        packed = dot(normed[...], ar_ref[...]).T
        lowrank = packed[: 3 * COLS]
        gates = jnp.concatenate(
            [gates_of(packed[place : place + COLS]) for place in range(3 * COLS, 6 * COLS, COLS)],
            axis=0,
        )
        zg_ref[: 3 * COLS] = lowrank
        zg_ref[3 * COLS :] = gates
        stores[5].start()
        mixed = pad_rows(lowrank * gates, LANES).astype(BF16).T
        for part in range(3):
            columns = slice(part * D, (part + 1) * D)
            value = dense[:, columns] + dot(mixed, b_ref[:, columns])
            if part == 0:
                qt_ref[...] = (value * QUERY_SCALE).astype(BF16).T
                stores[0].start()
            else:
                low = value.astype(BF16)
                natural, turned = ((k_ref, kt_ref), (v_ref, vt_ref))[part - 1]
                natural[...] = low
                turned[...] = low.T
                stores[2 * part - 1].start()
                stores[2 * part].start()

    first[0]()
    rest[0]()
    for load in loads:
        load.wait()
    dense_tile(0)
    first[1]()
    rest[1]()
    dense_tile(1)
    first[2]()
    buckets = buckets_ref[...]
    hits = jnp.where(row_iota((table_ref.shape[1], buckets.shape[1])) == buckets, LOG2E, 0.0)
    off_ref[...] = lax.dot_general(
        table_ref[...],
        hits,
        (((1,), (0,)), ((), ())),
        preferred_element_type=F32,
        precision=lax.Precision.HIGHEST,
    )
    first[3]()
    rest[2]()
    first[4]()
    for index in range(-(-FIRST_COUNT // count)):
        align_in(flat, shard_of(index).astype(F32), index * count)
    unpack_first(flat, ar_ref, b_ref, down, router)
    rest[3]()
    project()
    rest[4]()
    for index in range(FIRST_COUNT // count, PARAM_ROWS * LANES // count):
        align_in(flat, shard_of(index).astype(F32), index * count)
    unpack_rest(flat, rest_refs, work)
    for store in stores:
        store.wait()


def start(x, gain, w_qkv, shard, buckets, rel_table, count, axes, sizes, spans):
    length = x.shape[0]
    groups = sizes[0] * sizes[1] // 8
    link = (axes, sizes, spans) if groups else None
    rest_shapes = [
        shape for fan_in, fan_out in FANS[3:] for shape in ((fan_in, LANES), (LANES, fan_out))
    ]
    wide = [
        ((D, length), BF16),
        ((length, D), BF16),
        ((D, length), BF16),
        ((length, D), BF16),
        ((D, length), BF16),
        ((6 * COLS, length), F32),
    ]
    small = [
        ((HEADS, buckets.shape[1]), F32),
        ((D, 2 * LANES), BF16),
        ((LANES, 3 * D), BF16),
    ] + [(shape, BF16) for shape in rest_shapes]
    scratch = [
        pltpu.VMEM(x.shape, BF16),
        pltpu.VMEM(w_qkv.shape, BF16),
        pltpu.VMEM(x.shape, BF16),
        pltpu.VMEM((length, 3 * D), F32),
    ]
    scratch += [pltpu.VMEM(*member) for member in wide]
    scratch += [
        pltpu.VMEM((flat_rows(count), LANES), F32),
        pltpu.VMEM((D, LANES), F32),
        pltpu.VMEM((D, LANES), F32),
        pltpu.VMEM((SINGLE_BLOCKS * D, LANES), F32),
        pltpu.SemaphoreType.DMA((2,)),
        pltpu.SemaphoreType.DMA((len(wide),)),
    ]
    if link:
        scratch += [pltpu.VMEM((end - begin, 8, *shard.shape), BF16) for begin, end in spans]
        scratch += gather_semaphores(groups) * 2
    vmem = pl.BlockSpec(memory_space=pltpu.VMEM)
    anywhere = pl.BlockSpec(memory_space=pl.ANY)
    return pl.pallas_call(
        functools.partial(start_kernel, link, count),
        in_specs=[vmem] * 4 + [anywhere] * 2,
        out_specs=[anywhere] * len(wide) + [vmem] * len(small),
        out_shape=[jax.ShapeDtypeStruct(*member) for member in wide + small],
        scratch_shapes=scratch,
        compiler_params=params(collective_id=0, has_side_effects=True) if link else params(),
        name="start",
    )(shard, buckets, rel_table, gain, x, w_qkv)


def reduce_phases(ring, span, parts_ref, boxes, greets, sums_ref=None, sum_boxes=None):
    begin, end = span
    outbox, inbox, half, own, far_out, far_in, out_ref = boxes
    groups = ring.groups
    inside = (ring.group >= begin) & (ring.group < end)
    core_parts = (ring.first, ring.both, ring.second, ring.low)
    near = [ring.mate] * 4 + [ring.second, ring.second, ring.first]

    def push(slot):
        return ring.copy(slot, outbox.at[slot], inbox.at[slot], ring.device(ring.group, near[slot]))

    def fill(slot, value):
        outbox[slot] = value.astype(BF16)
        push(slot).start()

    def around(group):
        return ring.copy(
            7 + group - begin,
            far_out.at[group - begin],
            far_in.at[ring.group],
            ring.device(group, ring.low),
            7 + ring.group,
        )

    def arrived(group):
        return ring.copy(
            7,
            far_out.at[0],
            far_in.at[group],
            ring.device(group, ring.low),
            7 + group,
        )

    base = 7 + groups
    sum_peers = (ring.mate, ring.over_x, ring.over_y)

    def push_sums(slot):
        near_out, near_in = sum_boxes
        return ring.copy(
            base + slot,
            near_out.at[slot],
            near_in.at[slot],
            ring.device(ring.group, sum_peers[slot]),
        )

    def around_sums(step):
        near_out, near_in = sum_boxes
        target = (ring.group + step) % groups
        return ring.copy(
            base + 2 + step,
            near_out.at[3],
            near_in.at[3 + ring.group],
            ring.device(target, ring.low),
        )

    def start_sums(slot, value):
        if sum_boxes is not None:
            sum_boxes[0][slot] = value
            push_sums(slot).start()

    def phase0():
        if greets:
            ring.greet()
        if sum_boxes is not None:
            start_sums(0, sums_ref[...])
        for slot, part in enumerate(core_parts):
            fill(slot, parts_ref[:, part + ring.other])

    def phase1():
        push(0).wait()
        fill(4, parts_ref[:, ring.second] + inbox[0].astype(F32))
        push(1).wait()
        fill(5, parts_ref[:, ring.both] + inbox[1].astype(F32))
        if sum_boxes is not None:
            push_sums(0).wait()
            start_sums(1, sum_boxes[0][0] + sum_boxes[1][0])
        push(2).wait()
        half[...] = parts_ref[:, ring.first] + inbox[2].astype(F32)
        push(3).wait()
        own[...] = parts_ref[:, ring.low] + inbox[3].astype(F32)

    def phase2():
        push(5).wait()
        fill(6, half[...] + inbox[5].astype(F32))
        if sum_boxes is not None:
            push_sums(1).wait()
            start_sums(2, sum_boxes[0][1] + sum_boxes[1][1])
        push(4).wait()
        own[...] = own[...] + inbox[4].astype(F32)

    def phase3():
        push(6).wait()
        own[...] = own[...] + inbox[6].astype(F32)
        far_out[...] = own[...].astype(BF16)
        for group in range(begin, end):

            @pl.when(ring.group != group)
            def _():
                around(group).start()

        if sum_boxes is not None:
            near_out, near_in = sum_boxes
            push_sums(2).wait()
            near_out[3] = near_out[2] + near_in[2]
            for step in range(1, groups):
                around_sums(step).start()
            near_in[3 + ring.group] = near_out[3]

    def phase4(finish_sums=None):
        for group in range(begin, end):

            @pl.when(ring.group != group)
            def _():
                around(group).wait_send()

        @pl.when(inside)
        def _():
            for group in range(groups):

                @pl.when(ring.group != group)
                def _():
                    arrived(group).wait_recv()

            total = own[ring.group - begin]
            for step in range(1, groups):
                total = total + far_in[(ring.group + step) % groups].astype(F32)
            out_ref[...] = total

        if sum_boxes is not None:
            near_out, near_in = sum_boxes
            for step in range(1, groups):
                around_sums(step).wait()
            whole_sum = near_in[3]
            for index in range(1, groups):
                whole_sum = whole_sum + near_in[3 + index]
            finish_sums(whole_sum)

    return phase0, phase1, phase2, phase3, phase4


def reduce_scratch(groups, count, rows):
    return [
        pltpu.VMEM((7, count, rows, LANES), BF16),
        pltpu.VMEM((7, count, rows, LANES), BF16),
        pltpu.VMEM((count, rows, LANES), F32),
        pltpu.VMEM((count, rows, LANES), F32),
        pltpu.VMEM((count, rows, LANES), BF16),
        pltpu.VMEM((groups, rows, LANES), BF16),
    ]


def finish_kernel(link, count, dar_ref, db_ref, *refs):
    grads, sums_ref = refs[:6], refs[6]
    out_ref, roots_ref, flat, down, router, work, *more = refs[7:]

    def finish_sums(total):
        roots_ref[...] = jnp.sqrt(total / (total[:, 4:5] * D))

    assemble_rest(flat, grads, work)
    if link is None:
        assemble_first(flat, dar_ref, db_ref, down, router)
        out_ref[...] = align_out(flat, out_ref.shape[0], 0)
        finish_sums(sums_ref[...])
        return
    axes, sizes, spans = link
    parts_a, parts_b, near_out, near_in, *more = more
    boxes_a, boxes_b, sems = more[:7], more[7:14], more[14:]
    rows = out_ref.shape[0]
    split = spans[1][0]

    def align(parts, span):
        for group in range(*span):
            for low in range(8):
                parts[group - span[0], low] = align_out(flat, rows, (8 * group + low) * count)

    ring = Ring(axes, sizes, sems[0], sems[1])
    rest = reduce_phases(ring, spans[1], parts_b, boxes_b, True, sums_ref, (near_out, near_in))
    first = reduce_phases(
        Ring(axes, sizes, sems[2], sems[3]), spans[0], parts_a, boxes_a, False
    )
    align(parts_b, spans[1])
    rest[0]()
    assemble_first(flat, dar_ref, db_ref, down, router)
    align(parts_a, spans[0])
    first[0]()
    for step in range(1, 4):
        rest[step]()
        first[step]()
    rest[4](finish_sums)
    first[4]()

    @pl.when(ring.group < split)
    def _():
        out_ref[...] = boxes_a[6][...]

    @pl.when(ring.group >= split)
    def _():
        out_ref[...] = boxes_b[6][...]


def finish(dar, db, grads, sums, count, axes, sizes, spans):
    rows = shard_rows(count)
    groups = sizes[0] * sizes[1] // 8
    link = (axes, sizes, spans) if groups else None
    scratch = [
        pltpu.VMEM((flat_rows(count), LANES), F32),
        pltpu.VMEM((D, LANES), F32),
        pltpu.VMEM((D, LANES), F32),
        pltpu.VMEM((SINGLE_BLOCKS * D, LANES), F32),
    ]
    if link:
        widths = [end - begin for begin, end in spans]
        scratch += [pltpu.VMEM((width, 8, rows, LANES), F32) for width in widths]
        scratch += [
            pltpu.VMEM((4, *sums.shape), F32),
            pltpu.VMEM((3 + groups, *sums.shape), F32),
        ]
        for width in widths:
            scratch += reduce_scratch(groups, width, rows) + [pltpu.VMEM((rows, LANES), F32)]
        scratch += [pltpu.SemaphoreType.DMA((10 + 2 * groups,))] * 4
    vmem = pl.BlockSpec(memory_space=pltpu.VMEM)
    return pl.pallas_call(
        functools.partial(finish_kernel, link, count),
        in_specs=[vmem] * (3 + len(grads)),
        out_specs=[vmem] * 2,
        out_shape=[
            jax.ShapeDtypeStruct((rows, LANES), F32),
            jax.ShapeDtypeStruct(sums.shape, F32),
        ],
        scratch_shapes=scratch,
        compiler_params=params(collective_id=1, has_side_effects=True) if link else params(),
        name="finish",
    )(dar, db, *grads, sums)


def per_device(
    tokens,
    lengths,
    buckets,
    rel_table,
    gain_attn,
    gain_ff,
    w_qkv,
    w_out,
    w_in,
    w_down,
    adapters,
    cotangent,
    axes,
    sizes,
):
    seq_count, length, width = tokens.shape
    x = tokens.reshape(length, width)
    cot = cotangent.reshape(length, width)
    devices = sizes[0] * sizes[1]
    count = adapters.shape[0]
    rows = shard_rows(count)
    shard = jnp.pad(adapters, (0, rows * LANES - count)).reshape(rows, LANES)
    groups = devices // 8
    split_groups = min(-(-FIRST_COUNT // (8 * count)), max(groups - 1, 1))
    spans = ((0, split_groups), (split_groups, groups))
    reversed_buckets = jnp.pad(buckets[::-1], (0, 1)).reshape(1, 2 * length)
    qt, k, kt, v, vt, zg, offsets, ar_qkv, b_qkv, *packed = start(
        x, gain_attn, w_qkv, shard, reversed_buckets, rel_table.T, count, axes, sizes, spans
    )
    ot, lse = attend(lengths, offsets, qt, k, kt, vt)
    block_out, dmid, gt, sums, *grads = middle_part(
        lengths, ot, x, cot, gain_ff, w_out, w_in, w_down, packed
    )
    tokens_grad, dar_qkv, db_qkv = back_part(
        lengths,
        offsets,
        qt,
        k,
        kt,
        v,
        ot,
        gt,
        lse,
        x,
        gain_attn,
        w_qkv,
        ar_qkv,
        b_qkv,
        zg,
        dmid,
    )
    mine, roots = finish(dar_qkv, db_qkv, grads, sums, count, axes, sizes, spans)
    grad_shard = mine.reshape(-1)[:count]
    root_squares = roots[0, :4]
    return (
        block_out.reshape(tokens.shape),
        tokens_grad.reshape(tokens.shape),
        grad_shard,
        root_squares,
    )


def solution(mesh):
    axes = tuple(mesh.axis_names)
    sizes = tuple(mesh.shape[axis] for axis in axes)
    sequence = P(axes, None, None)
    placed = (
        sequence,
        P(axes),
        P(),
        P(),
        P(),
        P(),
        P(),
        P(),
        P(),
        P(),
        P(axes),
        sequence,
    )
    return jax.shard_map(
        functools.partial(per_device, axes=axes, sizes=sizes),
        mesh=mesh,
        in_specs=placed,
        out_specs=(sequence, sequence, P(axes), P()),
        check_vma=False,
    )
```

profile of v0, /device:TPU:0, one launch (start us, length us, event | category | flops | bytes accessed | tf_op | source)
XLA Modules:
  0.0 169.6 jit_solution(16682432538982851951)
XLA Ops:
  1.3 0.8 reverse
  2.0 0.1 slice.10
  2.1 0.6 pad.9
  2.7 1.4 pad_bitcast_fusion.shard_ref
  4.1 29.4 %start.1 = (bf16[768,1024]{1,0:T(8,128)(2,1)}, bf16[1024,768]{1,0:T(8,128)(2,1)}, bf16[768,1024]{1,0:T(8,128)(2,1)}, bf16[1024,768]{1,0:T(8,128)(2,1)}, bf16[768...) custom-call(bf16[160,128]{1,0:T(8,128)(2,1)} %pad_bitcast_fusion.sha, ...), custom_call_target="tpu_custom_call" | custom-call | tf_op jit(solution)/shard_map/start/pallas_call | solution.py:1213
  33.5 16.3 %attend.1 = (bf16[768,1024]{1,0:T(8,128)(2,1)}, f32[6,2,1024]{2,1,0:T(2,128)}) custom-call(s32[1]{0:T(128)S(6)} %copy.16.length_ref.refs_0_, f32[12,2048]{1,0:T(8,128)} %get-tuple-element.36.off_ref.refs_1_, bf16[768,1024]{1,0:T(8,128)(2,1)} %get-tuple-element.37.qt_ref.refs_2_, bf16[1024,768]{1,0:T(8,128)(2,1)} %get-tuple-element.38.k_ref.refs_3_, ...), custom_call_target="tpu_custom_call" | custom-call | tf_op jit(solution)/shard_map/attend/pallas_call | solution.py:251
  49.8 45.7 %middle_part.1 = (bf16[1024,768]{1,0:T(8,128)(2,1)}, f32[1024,768]{1,0:T(8,128)}, bf16[768,1024]{1,0:T(8,128)(2,1)}, f32[8,128]{1,0:T(8,128)}, f32[80,768]{1,0:T...) custom-call(s32[1]{0:T(128)S(6)} %copy.16.length_ref.refs_0_, ...), custom_call_target="tpu_custom_call" | custom-call | tf_op jit(solution)/shard_map/middle_part/pallas_call | solution.py:450
  95.5 44.9 %back_part.1 = (f32[1024,768]{1,0:T(8,128)}, f32[256,768]{1,0:T(8,128)}, f32[128,2304]{1,0:T(8,128)}) custom-call(s32[1]{0:T(128)S(6)} %copy.16.length_ref.refs_0_, f32[12,2048]{1,0:T(8,128)} %get-tuple-element.36.off_ref.refs_1_, bf16[768,1024]{1,0:T(8,128)(2,1)} %get-tuple-element.37.qt_ref.refs_2_, bf16[1024,768]{1,0:T(8,128)(2,1)} %get-tuple-element.38.k_ref.refs_3_, ...), custom_call_target="tpu_custom_call" | custom-call | tf_op jit(solution)/shard_map/back_part/pallas_call | solution.py:630
  140.4 26.5 %finish.1 = (f32[160,128]{1,0:T(8,128)}, f32[8,128]{1,0:T(8,128)}) custom-call(f32[256,768]{1,0:T(8,128)} %get-tuple-element.57.dar_ref, f32[128,2304]{1,0:T(8,128)} %get-tuple-element.58.db_ref, f32[80,768]{1,0:T(8,128)} %get-tuple-element.59.refs_0_, f32[48,768]{1,0:T(8,128)} %get-tuple-element.60.refs_1_, f32[80,768]{1,0:T(8,128)} %get-tuple-element.61.refs_2_, ...), custom_call_target="tpu_custom_call" | custom-call | tf_op jit(solution)/shard_map/finish/pallas_call | solution.py:1445
  166.9 1.5 slice.8
  168.4 1.2 slice_bitcast_fusion
where the time goes:
time: 170 us
  Pallas kernels  163 us (96%)
  local copies, waits for them, and re-layouts  5.55 us (3%)
    pallas_call x1, Pallas kernels, middle_part(): pl.pallas_call(middle_kernel, grid=(length // MIDDLE_ROWS,), in_specs=[pl...  45.7 us
    pallas_call x1, Pallas kernels, back_part(): pl.pallas_call(back_kernel, grid=(pairs + length // ROWS,), in_specs=[pl....  44.9 us
    pallas_call x1, Pallas kernels, start(): pl.pallas_call(functools.partial(start_kernel, link, count), in_specs=[vm...  29.4 us
    pallas_call x1, Pallas kernels, finish(): pl.pallas_call(functools.partial(finish_kernel, link, count), in_specs=[v...  26.5 us
    pallas_call x1, Pallas kernels, attend(): pl.pallas_call(attend_kernel, grid=(HEADS // 2,), in_specs=[pl.BlockSpec(...  16.3 us

commit v1 on v0

--- a/solution.py
+++ b/solution.py
@@ -47,6 +47,16 @@
 
 def dot_tn(a, b):
     return lax.dot_general(a, b, (((0,), (0,)), ((), ())), preferred_element_type=F32)
+
+
+def exact_dot(a, b):
+    return lax.dot_general(
+        a,
+        b,
+        (((1,), (0,)), ((), ())),
+        preferred_element_type=F32,
+        precision=lax.Precision.HIGHEST,
+    )
 
 
 def lane_iota(shape):
@@ -510,14 +520,20 @@
         grads = join_rows(
             gt_ref[half, :], extra_rows([-part for part in split_three(delta)]), odd
         )
+        query_blocks = []
+        previous = None
         for start in range(0, length, QBLOCK):
             columns = slice(start, start + QBLOCK)
-            scores = add_bias(dot(keys, queries[:, columns]), table.at[odd], start, length)
-            weights = jnp.exp2(scores)
+            raw = dot(keys, queries[:, columns])
+            grad_raw = dot(values, grads[:, columns])
+            if previous is not None:
+                query_blocks.append(dot(kt_ref[half, :], previous))
+            weights = jnp.exp2(add_bias(raw, table.at[odd], start, length))
             weights_all[:, columns] = weights.astype(BF16)
-            grad_scores = weights * dot(values, grads[:, columns])
-            grads_all[:, columns] = grad_scores.astype(BF16)
-        grad_query_parts.append(dot(kt_ref[half, :], grads_all[...]) * 0.125)
+            previous = (weights * grad_raw).astype(BF16)
+            grads_all[:, columns] = previous
+        query_blocks.append(dot(kt_ref[half, :], previous))
+        grad_query_parts.append(jnp.concatenate(query_blocks, axis=1) * 0.125)
         grad_values = dot_nt(weights_all[...], gt_ref[...])
         grad_keys = dot_nt(grads_all[...], qt_ref[...]) * LN2
         if odd:
@@ -915,10 +931,14 @@
 
 
 def greet(peers):
-    barrier = pltpu.get_barrier_semaphore()
     for peer in peers:
-        pl.semaphore_signal(barrier, inc=1, device_id=peer, device_id_type=MESH)
-    pl.semaphore_wait(barrier, len(peers))
+        pl.semaphore_signal(
+            pltpu.get_barrier_semaphore(), inc=1, device_id=peer, device_id_type=MESH
+        )
+
+
+def await_greetings(count):
+    pl.semaphore_wait(pltpu.get_barrier_semaphore(), count)
 
 
 class Ring:
@@ -943,6 +963,9 @@
         peers += [self.device(self.group, low) for low in (self.first, self.second, self.mate)]
         greet(peers)
 
+    def await_greetings(self):
+        await_greetings(self.groups + 2)
+
     def copy(self, slot, source, target, peer, arrival=None):
         return pltpu.make_async_remote_copy(
             src_ref=source,
@@ -999,6 +1022,7 @@
     def phase0():
         if greets:
             ring.greet()
+            ring.await_greetings()
 
         @pl.when(inside)
         def _():
@@ -1064,7 +1088,7 @@
     x_ref, w_ref, normed, dense = refs[15:19]
     outs = refs[19:25]
     qt_ref, k_ref, kt_ref, v_ref, vt_ref, zg_ref = outs
-    flat, down, router, work, loaded, stored, *more = refs[25:]
+    flat, down, router, work, offsets_ref, loaded, stored, *more = refs[25:]
     loads = [
         pltpu.make_async_copy(x_hbm, x_ref, loaded.at[0]),
         pltpu.make_async_copy(w_hbm, w_ref, loaded.at[1]),
@@ -1145,15 +1169,17 @@
     rest[1]()
     dense_tile(1)
     first[2]()
-    buckets = buckets_ref[...]
+    buckets = buckets_ref[...].reshape(1, buckets_ref.shape[0])
     hits = jnp.where(row_iota((table_ref.shape[1], buckets.shape[1])) == buckets, LOG2E, 0.0)
-    off_ref[...] = lax.dot_general(
-        table_ref[...],
-        hits,
-        (((1,), (0,)), ((), ())),
-        preferred_element_type=F32,
-        precision=lax.Precision.HIGHEST,
-    )
+    offsets_ref[...] = jnp.zeros_like(offsets_ref)
+    offsets_ref[:, : buckets.shape[1]] = exact_dot(table_ref[...], hits)
+    flip = (row_iota((LANES, LANES)) + lane_iota((LANES, LANES)) == LANES - 1).astype(F32)
+    blocks = offsets_ref.shape[1] // LANES
+    for block in range(blocks):
+        lanes = slice(block * LANES, (block + 1) * LANES)
+        turned = slice((blocks - 1 - block) * LANES, (blocks - block) * LANES)
+        off_ref[:, turned] = exact_dot(offsets_ref[:, lanes], flip)
+    off_ref[...] = pltpu.roll(off_ref[...], offsets_ref.shape[1] - 1, 1)
     first[3]()
     rest[2]()
     first[4]()
@@ -1186,7 +1212,7 @@
         ((6 * COLS, length), F32),
     ]
     small = [
-        ((HEADS, buckets.shape[1]), F32),
+        ((HEADS, 2 * length), F32),
         ((D, 2 * LANES), BF16),
         ((LANES, 3 * D), BF16),
     ] + [(shape, BF16) for shape in rest_shapes]
@@ -1202,6 +1228,7 @@
         pltpu.VMEM((D, LANES), F32),
         pltpu.VMEM((D, LANES), F32),
         pltpu.VMEM((SINGLE_BLOCKS * D, LANES), F32),
+        pltpu.VMEM((HEADS, 2 * length), F32),
         pltpu.SemaphoreType.DMA((2,)),
         pltpu.SemaphoreType.DMA((len(wide),)),
     ]
@@ -1283,7 +1310,7 @@
 
     def phase0():
         if greets:
-            ring.greet()
+            ring.await_greetings()
         if sum_boxes is not None:
             start_sums(0, sums_ref[...])
         for slot, part in enumerate(core_parts):
@@ -1297,6 +1324,8 @@
         if sum_boxes is not None:
             push_sums(0).wait()
             start_sums(1, sum_boxes[0][0] + sum_boxes[1][0])
+
+    def add1():
         push(2).wait()
         half[...] = parts_ref[:, ring.first] + inbox[2].astype(F32)
         push(3).wait()
@@ -1308,6 +1337,8 @@
         if sum_boxes is not None:
             push_sums(1).wait()
             start_sums(2, sum_boxes[0][1] + sum_boxes[1][1])
+
+    def add2():
         push(4).wait()
         own[...] = own[...] + inbox[4].astype(F32)
 
@@ -1358,7 +1389,7 @@
                 whole_sum = whole_sum + near_in[3 + index]
             finish_sums(whole_sum)
 
-    return phase0, phase1, phase2, phase3, phase4
+    return phase0, phase1, add1, phase2, add2, phase3, phase4
 
 
 def reduce_scratch(groups, count, rows):
@@ -1379,15 +1410,18 @@
     def finish_sums(total):
         roots_ref[...] = jnp.sqrt(total / (total[:, 4:5] * D))
 
+    if link is not None:
+        axes, sizes, spans = link
+        parts_a, parts_b, near_out, near_in, *more = more
+        boxes_a, boxes_b, sems = more[:7], more[7:14], more[14:]
+        ring = Ring(axes, sizes, sems[0], sems[1])
+        ring.greet()
     assemble_rest(flat, grads, work)
     if link is None:
         assemble_first(flat, dar_ref, db_ref, down, router)
         out_ref[...] = align_out(flat, out_ref.shape[0], 0)
         finish_sums(sums_ref[...])
         return
-    axes, sizes, spans = link
-    parts_a, parts_b, near_out, near_in, *more = more
-    boxes_a, boxes_b, sems = more[:7], more[7:14], more[14:]
     rows = out_ref.shape[0]
     split = spans[1][0]
 
@@ -1396,7 +1430,6 @@
             for low in range(8):
                 parts[group - span[0], low] = align_out(flat, rows, (8 * group + low) * count)
 
-    ring = Ring(axes, sizes, sems[0], sems[1])
     rest = reduce_phases(ring, spans[1], parts_b, boxes_b, True, sums_ref, (near_out, near_in))
     first = reduce_phases(
         Ring(axes, sizes, sems[2], sems[3]), spans[0], parts_a, boxes_a, False
@@ -1404,13 +1437,17 @@
     align(parts_b, spans[1])
     rest[0]()
     assemble_first(flat, dar_ref, db_ref, down, router)
+    rest[1]()
     align(parts_a, spans[0])
     first[0]()
-    for step in range(1, 4):
+    rest[2]()
+    for step in (1, 2):
+        first[step]()
+    for step in (3, 4, 5):
         rest[step]()
         first[step]()
-    rest[4](finish_sums)
-    first[4]()
+    rest[6](finish_sums)
+    first[6]()
 
     @pl.when(ring.group < split)
     def _():
@@ -1482,9 +1519,8 @@
     groups = devices // 8
     split_groups = min(-(-FIRST_COUNT // (8 * count)), max(groups - 1, 1))
     spans = ((0, split_groups), (split_groups, groups))
-    reversed_buckets = jnp.pad(buckets[::-1], (0, 1)).reshape(1, 2 * length)
     qt, k, kt, v, vt, zg, offsets, ar_qkv, b_qkv, *packed = start(
-        x, gain_attn, w_qkv, shard, reversed_buckets, rel_table.T, count, axes, sizes, spans
+        x, gain_attn, w_qkv, shard, buckets, rel_table.T, count, axes, sizes, spans
     )
     ot, lse = attend(lengths, offsets, qt, k, kt, vt)
     block_out, dmid, gt, sums, *grads = middle_part(

time: 170 us -> 165 us (0.971)
  Pallas kernels: 163 us -> 160 us
    pallas_call x1, Pallas kernels: 26.5 us -> 23.7 us  [finish(): pl.pallas_call(functools.partial(finish_kernel, link, count), in_specs=[v...]
where the time goes in v1:
time: 165 us
  Pallas kernels  160 us (97%)
  local copies, waits for them, and re-layouts  4.1 us (2%)
    pallas_call x1, Pallas kernels, middle_part(): pl.pallas_call(middle_kernel, grid=(length // MIDDLE_ROWS,), in_specs=[pl...  45.7 us
    pallas_call x1, Pallas kernels, back_part(): pl.pallas_call(back_kernel, grid=(pairs + length // ROWS,), in_specs=[pl....  44.4 us
    pallas_call x1, Pallas kernels, start(): pl.pallas_call(functools.partial(start_kernel, link, count), in_specs=[vm...  29.4 us
    pallas_call x1, Pallas kernels, finish(): pl.pallas_call(functools.partial(finish_kernel, link, count), in_specs=[v...  23.7 us
    pallas_call x1, Pallas kernels, attend(): pl.pallas_call(attend_kernel, grid=(HEADS // 2,), in_specs=[pl.BlockSpec(...  16.3 us

profile of v1, /device:TPU:0, one launch (start us, length us, event | category | flops | bytes accessed | tf_op | source)
XLA Modules:
  0.0 165.0 jit_solution(13807808694203394364)
XLA Ops:
  1.3 1.4 pad_bitcast_fusion.shard_ref
  2.7 29.4 %start.1 = (bf16[768,1024]{1,0:T(8,128)(2,1)}, bf16[1024,768]{1,0:T(8,128)(2,1)}, bf16[768,1024]{1,0:T(8,128)(2,1)}, bf16[1024,768]{1,0:T(8,128)(2,1)}, bf16[768...) custom-call(bf16[160,128]{1,0:T(8,128)(2,1)} %pad_bitcast_fusion.sha, ...), custom_call_target="tpu_custom_call" | custom-call | tf_op jit(solution)/shard_map/start/pallas_call | solution.py:1240
  32.1 16.3 %attend.1 = (bf16[768,1024]{1,0:T(8,128)(2,1)}, f32[6,2,1024]{2,1,0:T(2,128)}) custom-call(s32[1]{0:T(128)S(6)} %copy.16.length_ref.refs_0_, f32[12,2048]{1,0:T(8,128)} %get-tuple-element.36.off_ref.refs_1_, bf16[768,1024]{1,0:T(8,128)(2,1)} %get-tuple-element.37.qt_ref.refs_2_, bf16[1024,768]{1,0:T(8,128)(2,1)} %get-tuple-element.38.k_ref.refs_3_, ...), custom_call_target="tpu_custom_call" | custom-call | tf_op jit(solution)/shard_map/attend/pallas_call | solution.py:261
  48.4 45.7 %middle_part.1 = (bf16[1024,768]{1,0:T(8,128)(2,1)}, f32[1024,768]{1,0:T(8,128)}, bf16[768,1024]{1,0:T(8,128)(2,1)}, f32[8,128]{1,0:T(8,128)}, f32[80,768]{1,0:T...) custom-call(s32[1]{0:T(128)S(6)} %copy.16.length_ref.refs_0_, ...), custom_call_target="tpu_custom_call" | custom-call | tf_op jit(solution)/shard_map/middle_part/pallas_call | solution.py:460
  94.1 44.4 %back_part.1 = (f32[1024,768]{1,0:T(8,128)}, f32[256,768]{1,0:T(8,128)}, f32[128,2304]{1,0:T(8,128)}) custom-call(s32[1]{0:T(128)S(6)} %copy.16.length_ref.refs_0_, f32[12,2048]{1,0:T(8,128)} %get-tuple-element.36.off_ref.refs_1_, bf16[768,1024]{1,0:T(8,128)(2,1)} %get-tuple-element.37.qt_ref.refs_2_, bf16[1024,768]{1,0:T(8,128)(2,1)} %get-tuple-element.38.k_ref.refs_3_, ...), custom_call_target="tpu_custom_call" | custom-call | tf_op jit(solution)/shard_map/back_part/pallas_call | solution.py:646
  138.5 23.7 %finish.1 = (f32[160,128]{1,0:T(8,128)}, f32[8,128]{1,0:T(8,128)}) custom-call(f32[256,768]{1,0:T(8,128)} %get-tuple-element.57.dar_ref, f32[128,2304]{1,0:T(8,128)} %get-tuple-element.58.db_ref, f32[80,768]{1,0:T(8,128)} %get-tuple-element.59.refs_0_, f32[48,768]{1,0:T(8,128)} %get-tuple-element.60.refs_1_, f32[80,768]{1,0:T(8,128)} %get-tuple-element.61.refs_2_, ...), custom_call_target="tpu_custom_call" | custom-call | tf_op jit(solution)/shard_map/finish/pallas_call | solution.py:1482
  162.2 1.5 slice.8
  163.8 1.2 slice_bitcast_fusion

commit v2 on v1

--- a/solution.py
+++ b/solution.py
@@ -1075,7 +1075,7 @@
 def start_kernel(
     link,
     count,
-    shard_ref,
+    values_ref,
     buckets_ref,
     table_ref,
     gain_ref,
@@ -1088,7 +1088,7 @@
     x_ref, w_ref, normed, dense = refs[15:19]
     outs = refs[19:25]
     qt_ref, k_ref, kt_ref, v_ref, vt_ref, zg_ref = outs
-    flat, down, router, work, offsets_ref, loaded, stored, *more = refs[25:]
+    flat, down, router, work, offsets_ref, shard_ref, loaded, stored, *more = refs[25:]
     loads = [
         pltpu.make_async_copy(x_hbm, x_ref, loaded.at[0]),
         pltpu.make_async_copy(w_hbm, w_ref, loaded.at[1]),
@@ -1099,6 +1099,9 @@
     ]
     for load in loads:
         load.start()
+    values = values_ref[...].astype(F32)
+    values = jnp.pad(values, (0, shard_ref.shape[0] * LANES - count))
+    shard_ref[...] = values.reshape(shard_ref.shape).astype(BF16)
     if link is None:
         first = [lambda: None] * 5
         rest = first
@@ -1229,11 +1232,13 @@
         pltpu.VMEM((D, LANES), F32),
         pltpu.VMEM((SINGLE_BLOCKS * D, LANES), F32),
         pltpu.VMEM((HEADS, 2 * length), F32),
+        pltpu.VMEM((shard_rows(count), LANES), BF16),
         pltpu.SemaphoreType.DMA((2,)),
         pltpu.SemaphoreType.DMA((len(wide),)),
     ]
     if link:
-        scratch += [pltpu.VMEM((end - begin, 8, *shard.shape), BF16) for begin, end in spans]
+        rows = shard_rows(count)
+        scratch += [pltpu.VMEM((end - begin, 8, rows, LANES), BF16) for begin, end in spans]
         scratch += gather_semaphores(groups) * 2
     vmem = pl.BlockSpec(memory_space=pltpu.VMEM)
     anywhere = pl.BlockSpec(memory_space=pl.ANY)
@@ -1408,7 +1413,7 @@
     out_ref, roots_ref, flat, down, router, work, *more = refs[7:]
 
     def finish_sums(total):
-        roots_ref[...] = jnp.sqrt(total / (total[:, 4:5] * D))
+        roots_ref[...] = jnp.sqrt(total / (total[:, 4:5] * D))[0, :4]
 
     if link is not None:
         axes, sizes, spans = link
@@ -1419,10 +1424,10 @@
     assemble_rest(flat, grads, work)
     if link is None:
         assemble_first(flat, dar_ref, db_ref, down, router)
-        out_ref[...] = align_out(flat, out_ref.shape[0], 0)
+        out_ref[...] = align_out(flat, shard_rows(count), 0).reshape(-1)[:count]
         finish_sums(sums_ref[...])
         return
-    rows = out_ref.shape[0]
+    rows = shard_rows(count)
     split = spans[1][0]
 
     def align(parts, span):
@@ -1451,11 +1456,11 @@
 
     @pl.when(ring.group < split)
     def _():
-        out_ref[...] = boxes_a[6][...]
+        out_ref[...] = boxes_a[6][...].reshape(-1)[:count]
 
     @pl.when(ring.group >= split)
     def _():
-        out_ref[...] = boxes_b[6][...]
+        out_ref[...] = boxes_b[6][...].reshape(-1)[:count]
 
 
 def finish(dar, db, grads, sums, count, axes, sizes, spans):
@@ -1484,8 +1489,8 @@
         in_specs=[vmem] * (3 + len(grads)),
         out_specs=[vmem] * 2,
         out_shape=[
-            jax.ShapeDtypeStruct((rows, LANES), F32),
-            jax.ShapeDtypeStruct(sums.shape, F32),
+            jax.ShapeDtypeStruct((count,), F32),
+            jax.ShapeDtypeStruct((4,), F32),
         ],
         scratch_shapes=scratch,
         compiler_params=params(collective_id=1, has_side_effects=True) if link else params(),
@@ -1514,13 +1519,11 @@
     cot = cotangent.reshape(length, width)
     devices = sizes[0] * sizes[1]
     count = adapters.shape[0]
-    rows = shard_rows(count)
-    shard = jnp.pad(adapters, (0, rows * LANES - count)).reshape(rows, LANES)
     groups = devices // 8
     split_groups = min(-(-FIRST_COUNT // (8 * count)), max(groups - 1, 1))
     spans = ((0, split_groups), (split_groups, groups))
     qt, k, kt, v, vt, zg, offsets, ar_qkv, b_qkv, *packed = start(
-        x, gain_attn, w_qkv, shard, buckets, rel_table.T, count, axes, sizes, spans
+        x, gain_attn, w_qkv, adapters, buckets, rel_table.T, count, axes, sizes, spans
     )
     ot, lse = attend(lengths, offsets, qt, k, kt, vt)
     block_out, dmid, gt, sums, *grads = middle_part(
@@ -1545,8 +1548,8 @@
         dmid,
     )
     mine, roots = finish(dar_qkv, db_qkv, grads, sums, count, axes, sizes, spans)
-    grad_shard = mine.reshape(-1)[:count]
-    root_squares = roots[0, :4]
+    grad_shard = mine
+    root_squares = roots
     return (
         block_out.reshape(tokens.shape),
         tokens_grad.reshape(tokens.shape),

time: 165 us -> 164 us (level)
    unnamed x0 -> x2, local copies, waits for them, and re-layouts: none -> 2.67 us
where the time goes in v2:
time: 164 us
  Pallas kernels  160 us (98%)
  local copies, waits for them, and re-layouts  2.67 us (2%)
    pallas_call x1, Pallas kernels, middle_part(): pl.pallas_call(middle_kernel, grid=(length // MIDDLE_ROWS,), in_specs=[pl...  45.7 us
    pallas_call x1, Pallas kernels, back_part(): pl.pallas_call(back_kernel, grid=(pairs + length // ROWS,), in_specs=[pl....  44.4 us
    pallas_call x1, Pallas kernels, start(): pl.pallas_call(functools.partial(start_kernel, link, count), in_specs=[vm...  29.5 us
    pallas_call x1, Pallas kernels, finish(): pl.pallas_call(functools.partial(finish_kernel, link, count), in_specs=[v...  23.7 us
    pallas_call x1, Pallas kernels, attend(): pl.pallas_call(attend_kernel, grid=(HEADS // 2,), in_specs=[pl.BlockSpec(...  16.3 us

profile of v2, /device:TPU:0, one launch (start us, length us, event | category | flops | bytes accessed | tf_op | source)
XLA Modules:
  0.0 163.6 jit_solution(5589320907738602890)
XLA Ops:
  1.3 29.5 %start.1 = (bf16[768,1024]{1,0:T(8,128)(2,1)}, bf16[1024,768]{1,0:T(8,128)(2,1)}, bf16[768,1024]{1,0:T(8,128)(2,1)}, bf16[1024,768]{1,0:T(8,128)(2,1)}, bf16[768...) custom-call(bf16[19440]{0:T(1024)(128)(2,1)} %values_ref.1, ...), custom_call_target="tpu_custom_call" | custom-call | tf_op jit(solution)/shard_map/start/pallas_call | solution.py:1245
  30.8 16.3 %attend.1 = (bf16[768,1024]{1,0:T(8,128)(2,1)}, f32[6,2,1024]{2,1,0:T(2,128)}) custom-call(s32[1]{0:T(128)S(6)} %copy.18.length_ref.refs_0_, f32[12,2048]{1,0:T(8,128)} %get-tuple-element.36.off_ref.refs_1_, bf16[768,1024]{1,0:T(8,128)(2,1)} %get-tuple-element.37.qt_ref.refs_2_, bf16[1024,768]{1,0:T(8,128)(2,1)} %get-tuple-element.38.k_ref.refs_3_, ...), custom_call_target="tpu_custom_call" | custom-call | tf_op jit(solution)/shard_map/attend/pallas_call | solution.py:261
  47.1 45.7 %middle_part.1 = (bf16[1024,768]{1,0:T(8,128)(2,1)}, f32[1024,768]{1,0:T(8,128)}, bf16[768,1024]{1,0:T(8,128)(2,1)}, f32[8,128]{1,0:T(8,128)}, f32[80,768]{1,0:T...) custom-call(s32[1]{0:T(128)S(6)} %copy.18.length_ref.refs_0_, ...), custom_call_target="tpu_custom_call" | custom-call | tf_op jit(solution)/shard_map/middle_part/pallas_call | solution.py:460
  92.8 44.4 %back_part.1 = (f32[1024,768]{1,0:T(8,128)}, f32[256,768]{1,0:T(8,128)}, f32[128,2304]{1,0:T(8,128)}) custom-call(s32[1]{0:T(128)S(6)} %copy.18.length_ref.refs_0_, f32[12,2048]{1,0:T(8,128)} %get-tuple-element.36.off_ref.refs_1_, bf16[768,1024]{1,0:T(8,128)(2,1)} %get-tuple-element.37.qt_ref.refs_2_, bf16[1024,768]{1,0:T(8,128)(2,1)} %get-tuple-element.38.k_ref.refs_3_, ...), custom_call_target="tpu_custom_call" | custom-call | tf_op jit(solution)/shard_map/back_part/pallas_call | solution.py:646
  137.2 23.7 %finish.1 = (f32[19440]{0:T(1024)}, f32[4]{0:T(128)}) custom-call(f32[256,768]{1,0:T(8,128)} %get-tuple-element.57.dar_ref, f32[128,2304]{1,0:T(8,128)} %get-tuple-element.58.db_ref, f32[80,768]{1,0:T(8,128)} %get-tuple-element.59.refs_0_, f32[48,768]{1,0:T(8,128)} %get-tuple-element.60.refs_1_, f32[80,768]{1,0:T(8,128)} %get-tuple-element.61.refs_2_, ...), custom_call_target="tpu_custom_call" | custom-call | tf_op jit(solution)/shard_map/finish/pallas_call | solution.py:1487
  160.9 1.5 copy.19
  162.5 1.1 copy.20

commit v3 on v2

--- a/solution.py
+++ b/solution.py
@@ -1498,6 +1498,23 @@
     )(dar, db, *grads, sums)
 
 
+def deliver_kernel(grads_ref, roots_ref, grads_out, roots_out):
+    grads_out[...] = grads_ref[...]
+    roots_out[...] = roots_ref[...]
+
+
+def deliver(grads, roots):
+    vmem = pl.BlockSpec(memory_space=pltpu.VMEM)
+    return pl.pallas_call(
+        deliver_kernel,
+        in_specs=[vmem] * 2,
+        out_specs=[vmem] * 2,
+        out_shape=[jax.ShapeDtypeStruct(member.shape, F32) for member in (grads, roots)],
+        compiler_params=params(),
+        name="deliver",
+    )(grads, roots)
+
+
 def per_device(
     tokens,
     lengths,
@@ -1547,7 +1564,9 @@
         zg,
         dmid,
     )
-    mine, roots = finish(dar_qkv, db_qkv, grads, sums, count, axes, sizes, spans)
+    mine, roots = deliver(
+        *finish(dar_qkv, db_qkv, grads, sums, count, axes, sizes, spans)
+    )
     grad_shard = mine
     root_squares = roots
     return (

time: 164 us -> 163 us (level)
  local copies, waits for them, and re-layouts: 2.67 us -> 0 us
    unnamed x2 -> x0, local copies, waits for them, and re-layouts: 2.67 us -> none
where the time goes in v3:
time: 163 us; the launch traced here: 162 us
  Pallas kernels  161 us (99%)
    pallas_call x1, Pallas kernels, middle_part(): pl.pallas_call(middle_kernel, grid=(length // MIDDLE_ROWS,), in_specs=[pl...  45.7 us
    pallas_call x1, Pallas kernels, back_part(): pl.pallas_call(back_kernel, grid=(pairs + length // ROWS,), in_specs=[pl....  44.4 us
    pallas_call x1, Pallas kernels, start(): pl.pallas_call(functools.partial(start_kernel, link, count), in_specs=[vm...  29.5 us
    pallas_call x1, Pallas kernels, finish(): pl.pallas_call(functools.partial(finish_kernel, link, count), in_specs=[v...  23.7 us
    pallas_call x1, Pallas kernels, attend(): pl.pallas_call(attend_kernel, grid=(HEADS // 2,), in_specs=[pl.BlockSpec(...  16.3 us

profile of v3, /device:TPU:0, one launch (start us, length us, event | category | flops | bytes accessed | tf_op | source)
XLA Modules:
  0.0 162.5 jit_solution(1293402754303550994)
XLA Ops:
  1.3 29.5 %start.1 = (bf16[768,1024]{1,0:T(8,128)(2,1)}, bf16[1024,768]{1,0:T(8,128)(2,1)}, bf16[768,1024]{1,0:T(8,128)(2,1)}, bf16[1024,768]{1,0:T(8,128)(2,1)}, bf16[768...) custom-call(bf16[19440]{0:T(1024)(128)(2,1)} %values_ref.1, ...), custom_call_target="tpu_custom_call" | custom-call | tf_op jit(solution)/shard_map/start/pallas_call | solution.py:1245
  30.8 16.3 %attend.1 = (bf16[768,1024]{1,0:T(8,128)(2,1)}, f32[6,2,1024]{2,1,0:T(2,128)}) custom-call(s32[1]{0:T(128)S(6)} %copy.16.length_ref.refs_0_, f32[12,2048]{1,0:T(8,128)} %get-tuple-element.38.off_ref.refs_1_, bf16[768,1024]{1,0:T(8,128)(2,1)} %get-tuple-element.39.qt_ref.refs_2_, bf16[1024,768]{1,0:T(8,128)(2,1)} %get-tuple-element.40.k_ref.refs_3_, ...), custom_call_target="tpu_custom_call" | custom-call | tf_op jit(solution)/shard_map/attend/pallas_call | solution.py:261
  47.1 45.7 %middle_part.1 = (bf16[1024,768]{1,0:T(8,128)(2,1)}, f32[1024,768]{1,0:T(8,128)}, bf16[768,1024]{1,0:T(8,128)(2,1)}, f32[8,128]{1,0:T(8,128)}, f32[80,768]{1,0:T...) custom-call(s32[1]{0:T(128)S(6)} %copy.16.length_ref.refs_0_, ...), custom_call_target="tpu_custom_call" | custom-call | tf_op jit(solution)/shard_map/middle_part/pallas_call | solution.py:460
  92.8 44.4 %back_part.1 = (f32[1024,768]{1,0:T(8,128)}, f32[256,768]{1,0:T(8,128)}, f32[128,2304]{1,0:T(8,128)}) custom-call(s32[1]{0:T(128)S(6)} %copy.16.length_ref.refs_0_, f32[12,2048]{1,0:T(8,128)} %get-tuple-element.38.off_ref.refs_1_, bf16[768,1024]{1,0:T(8,128)(2,1)} %get-tuple-element.39.qt_ref.refs_2_, bf16[1024,768]{1,0:T(8,128)(2,1)} %get-tuple-element.40.k_ref.refs_3_, ...), custom_call_target="tpu_custom_call" | custom-call | tf_op jit(solution)/shard_map/back_part/pallas_call | solution.py:646
  137.2 23.7 %finish.1 = (f32[19440]{0:T(1024)}, f32[4]{0:T(128)}) custom-call(f32[256,768]{1,0:T(8,128)} %get-tuple-element.59.dar_ref, f32[128,2304]{1,0:T(8,128)} %get-tuple-element.60.db_ref, f32[80,768]{1,0:T(8,128)} %get-tuple-element.61.refs_0_, f32[48,768]{1,0:T(8,128)} %get-tuple-element.62.refs_1_, f32[80,768]{1,0:T(8,128)} %get-tuple-element.63.refs_2_, ...), custom_call_target="tpu_custom_call" | custom-call | tf_op jit(solution)/shard_map/finish/pallas_call | solution.py:1487
  160.9 1.5 deliver.1

commit v4 on v3

--- a/solution.py
+++ b/solution.py
@@ -566,8 +566,9 @@
     grad_normed = jnp.zeros((ROWS, D), F32)
     for grad, lanes in zip(grads, columns):
         grad_normed = grad_normed + dot_nt(grad, w_ref[:, lanes])
+    turned = grad_mixed.T
+    for grad, lanes in zip(grads, columns):
         db_ref[:, lanes] += dot(mixed, grad)
-    turned = grad_mixed.T
     parts = []
     for first in range(0, 3 * COLS, COLS):
         place = slice(first, first + COLS)

time: 163 us -> 162 us (level)
  no operation moved by 1% of the time
where the time goes in v4:
time: 162 us
  Pallas kernels  161 us (99%)
    pallas_call x1, Pallas kernels, middle_part(): pl.pallas_call(middle_kernel, grid=(length // MIDDLE_ROWS,), in_specs=[pl...  45.7 us
    pallas_call x1, Pallas kernels, back_part(): pl.pallas_call(back_kernel, grid=(pairs + length // ROWS,), in_specs=[pl....  44.2 us
    pallas_call x1, Pallas kernels, start(): pl.pallas_call(functools.partial(start_kernel, link, count), in_specs=[vm...  29.5 us
    pallas_call x1, Pallas kernels, finish(): pl.pallas_call(functools.partial(finish_kernel, link, count), in_specs=[v...  23.7 us
    pallas_call x1, Pallas kernels, attend(): pl.pallas_call(attend_kernel, grid=(HEADS // 2,), in_specs=[pl.BlockSpec(...  16.3 us

profile of v4, /device:TPU:0, one launch (start us, length us, event | category | flops | bytes accessed | tf_op | source)
XLA Modules:
  0.0 162.2 jit_solution(2828079679071981951)
XLA Ops:
  1.3 29.5 %start.1 = (bf16[768,1024]{1,0:T(8,128)(2,1)}, bf16[1024,768]{1,0:T(8,128)(2,1)}, bf16[768,1024]{1,0:T(8,128)(2,1)}, bf16[1024,768]{1,0:T(8,128)(2,1)}, bf16[768...) custom-call(bf16[19440]{0:T(1024)(128)(2,1)} %values_ref.1, ...), custom_call_target="tpu_custom_call" | custom-call | tf_op jit(solution)/shard_map/start/pallas_call | solution.py:1246
  30.8 16.3 %attend.1 = (bf16[768,1024]{1,0:T(8,128)(2,1)}, f32[6,2,1024]{2,1,0:T(2,128)}) custom-call(s32[1]{0:T(128)S(6)} %copy.16.length_ref.refs_0_, f32[12,2048]{1,0:T(8,128)} %get-tuple-element.38.off_ref.refs_1_, bf16[768,1024]{1,0:T(8,128)(2,1)} %get-tuple-element.39.qt_ref.refs_2_, bf16[1024,768]{1,0:T(8,128)(2,1)} %get-tuple-element.40.k_ref.refs_3_, ...), custom_call_target="tpu_custom_call" | custom-call | tf_op jit(solution)/shard_map/attend/pallas_call | solution.py:261
  47.1 45.7 %middle_part.1 = (bf16[1024,768]{1,0:T(8,128)(2,1)}, f32[1024,768]{1,0:T(8,128)}, bf16[768,1024]{1,0:T(8,128)(2,1)}, f32[8,128]{1,0:T(8,128)}, f32[80,768]{1,0:T...) custom-call(s32[1]{0:T(128)S(6)} %copy.16.length_ref.refs_0_, ...), custom_call_target="tpu_custom_call" | custom-call | tf_op jit(solution)/shard_map/middle_part/pallas_call | solution.py:460
  92.8 44.2 %back_part.1 = (f32[1024,768]{1,0:T(8,128)}, f32[256,768]{1,0:T(8,128)}, f32[128,2304]{1,0:T(8,128)}) custom-call(s32[1]{0:T(128)S(6)} %copy.16.length_ref.refs_0_, f32[12,2048]{1,0:T(8,128)} %get-tuple-element.38.off_ref.refs_1_, bf16[768,1024]{1,0:T(8,128)(2,1)} %get-tuple-element.39.qt_ref.refs_2_, bf16[1024,768]{1,0:T(8,128)(2,1)} %get-tuple-element.40.k_ref.refs_3_, ...), custom_call_target="tpu_custom_call" | custom-call | tf_op jit(solution)/shard_map/back_part/pallas_call | solution.py:647
  137.0 23.7 %finish.1 = (f32[19440]{0:T(1024)}, f32[4]{0:T(128)}) custom-call(f32[256,768]{1,0:T(8,128)} %get-tuple-element.59.dar_ref, f32[128,2304]{1,0:T(8,128)} %get-tuple-element.60.db_ref, f32[80,768]{1,0:T(8,128)} %get-tuple-element.61.refs_0_, f32[48,768]{1,0:T(8,128)} %get-tuple-element.62.refs_1_, f32[80,768]{1,0:T(8,128)} %get-tuple-element.63.refs_2_, ...), custom_call_target="tpu_custom_call" | custom-call | tf_op jit(solution)/shard_map/finish/pallas_call | solution.py:1488
  160.7 1.5 deliver.1
